TPU v7x, 512 devices: a whole 4x8x8 slice. The times are simulated.
512 devices in a mesh: ia: 16 (over y_hi, x), ja: 16 (over z, core), vert: 2 (over y_lo).
Axes of the slice: x: 4, y: 8 (y_hi: 4, y_lo: 2; y = y_hi * 2 + y_lo), z: 8, core: 2. Of those that a mesh axis runs over, the one named last changes fastest.
Arguments:
- amplitudes: bfloat16 [16, 16, 2, 2, 3, 16384], P('ia', 'ja'), may hold values from -6 to 6
- tile_lists: int32 [16, 16, 3], P('ia', 'ja'), may hold values from 0 to 3, as said below
- integrals: bfloat16 [32, 256, 256], P('ia', 'vert'), may hold values from -0.1875 to 0.1875
- occupied_energy: float32 [32], replicated, may hold values from -2 to -0.5
- virtual_energy: float32 [256], replicated, may hold values from 0.5 to 4
Outputs:
- ladder_update: bfloat16 [16, 16, 2, 2, 256, 256], P('ia', 'ja', None, None, 'vert')
Inputs may be any that keep to these rules, and one draw needn't show every extreme that they name: `tile_lists`: the 3 entries of one pair block are distinct.
All inputs are finite; a program needn't handle non-finite values.
Results may differ from a plain program's by a relative error of at most 0.0049.
Values may be sent and summed in bfloat16 or wider, within the bound.
A program may use at most 64 MiB of HBM per device.

v0:
```python
import jax
import jax.numpy as jnp
from jax import lax
from jax.sharding import PartitionSpec as P

NT = 2


def partner_2(value, axis, distance):
    mask = 2**distance
    pairs = [(source, source ^ mask) for source in range(lax.axis_size(axis))]
    return lax.ppermute(value, axis, pairs)


def densify(amplitude_tiles, listing, width):
    pair_count = amplitude_tiles.shape[0]
    catalog = (listing[:, None] == jnp.arange(NT * NT, dtype=jnp.int32)[None, :]).astype(
        jnp.bfloat16
    )
    dense = jnp.einsum(
        "pkt,ks->pst", amplitude_tiles, catalog, preferred_element_type=jnp.float32
    ).astype(jnp.bfloat16)
    dense = dense.reshape(pair_count, NT, NT, width // NT, width // NT).transpose(0, 1, 3, 2, 4)
    return dense.reshape(pair_count, width, width)


def on_device(amplitudes, tile_lists, integrals, occupied_energy, virtual_energy):
    occ_tile = amplitudes.shape[2]
    listed = amplitudes.shape[4]
    tile_area = amplitudes.shape[5]
    pair_count = occ_tile * occ_tile
    width = virtual_energy.shape[0]
    half_rows = integrals.shape[1]
    row_tile = lax.axis_index("ia")
    code_tile = lax.axis_index("ja")
    parity = lax.axis_index("vert")
    own_first = parity == 0
    levels = lax.axis_size("ia").bit_length() - 1
    local_amps = amplitudes.reshape(pair_count, listed, tile_area)
    local_list = tile_lists.reshape(listed)
    dense = densify(local_amps, local_list, width)
    partner = partner_2(integrals, "vert", 0)

    def full_rows(mine, other):
        lower = jnp.where(own_first, mine, other)
        upper = jnp.where(own_first, other, mine)
        return jnp.concatenate([lower, upper], axis=0)

    own_zero = jnp.zeros((pair_count, half_rows, width), jnp.float32)

    def own_term(total, factor_pair):
        mine, other = factor_pair
        whole = full_rows(mine, other)
        inner = jnp.einsum("pcd,bd->pcb", dense, whole, preferred_element_type=jnp.float32).astype(
            jnp.bfloat16
        )
        return (
            total + jnp.einsum("ac,pcb->pab", mine, inner, preferred_element_type=jnp.float32),
            None,
        )

    result, _ = lax.scan(
        own_term,
        own_zero,
        (
            lax.all_gather(integrals, "ia", axis=0, tiled=True),
            lax.all_gather(partner, "ia", axis=0, tiled=True),
        ),
    )
    folded = result
    mirrored = folded
    for level in range(levels):
        other = partner_2(mirrored, "ia", level)
        take = jnp.bitwise_and(jnp.right_shift(code_tile, level), 1) == 1
        mirrored = jnp.where(take, other, mirrored)
    kept_cols = lax.dynamic_slice_in_dim(mirrored, parity * half_rows, half_rows, 2)
    sent_cols = lax.dynamic_slice_in_dim(mirrored, (1 - parity) * half_rows, half_rows, 2)
    came = partner_2(sent_cols, "vert", 0)
    lower = jnp.where(own_first, kept_cols, came)
    upper = jnp.where(own_first, came, kept_cols)
    mirror_part = jnp.concatenate([lower, upper], axis=1)
    turned = mirror_part.reshape(occ_tile, occ_tile, width, half_rows).transpose(1, 0, 3, 2)
    summed = folded.reshape(occ_tile, occ_tile, half_rows, width) + turned
    occ_i = lax.dynamic_slice_in_dim(occupied_energy, row_tile * occ_tile, occ_tile)
    occ_j = lax.dynamic_slice_in_dim(
        occupied_energy, jnp.bitwise_xor(row_tile, code_tile) * occ_tile, occ_tile
    )
    virt_rows = lax.dynamic_slice_in_dim(virtual_energy, parity * half_rows, half_rows)
    denom = (
        virt_rows[None, None, :, None]
        + virtual_energy[None, None, None, :]
        - (occ_i[:, None, None, None] + occ_j[None, :, None, None])
    )
    result = summed / denom
    return result.reshape(1, 1, occ_tile, occ_tile, half_rows, width).astype(jnp.bfloat16)


def solution(mesh):
    return jax.shard_map(
        on_device,
        mesh=mesh,
        in_specs=(
            P("ia", "ja", None, None, None, None),
            P("ia", "ja", None),
            P("ia", "vert", None),
            P(),
            P(),
        ),
        out_specs=P("ia", "ja", None, None, "vert", None),
        check_vma=False,
    )
```

profile of v0, /device:TPU:1, one launch (start us, length us, event | category | flops | bytes accessed | tf_op | source)
XLA Modules:
  0.0 323.2 jit_solution(16071705290770834402)
XLA Ops:
  7.3 4.0 %collective-permute-start = (bf16[2,128,256]{2,1,0:T(8,128)(2,1)}, bf16[2,128,256]{2,1,0:T(8,128)(2,1)S(1)}, u32[]{:S(2)}, u32[]{:S(2)}) collective-permute-start(bf16[2,128,256]{2,1,0:T(8,128)(2,1)} %param.9), channel_id=1, source_target_pairs={{0,1},{1,0},{2,3},{3,2},{4,5},{5,4},{6,7},{7,6},{8,9},{9,8},{10,11... | collective-permute-start | bytes 393224 | tf_op jit(solution)/shard_map/ppermute | solution.py:12
  11.3 2.6 collective-permute-done
  14.6 1.3 copy.28
  18.5 61.7 %all-gather.3.cloned.1.call-done = bf16[32,128,256]{2,1,0:T(8,128)(2,1)} async-done(((bf16[2,128,256]{2,1,0:T(8,128)(2,1)}), bf16[32,128,256]{2,1,0:T(8,128)(2,1)}) %all-gather.3.cloned.1.call-update) | async-done | bytes 2097168 | tf_op jit(solution)/shard_map/all_gather | solution.py:66
  80.2 65.2 %all-gather.5.cloned.1.call-done = bf16[32,128,256]{2,1,0:T(8,128)(2,1)} async-done(((bf16[2,128,256]{2,1,0:T(8,128)(2,1)}), bf16[32,128,256]{2,1,0:T(8,128)(2,1)}) %all-gather.5.cloned.1.call-update) | async-done | bytes 2097168 | tf_op jit(solution)/shard_map/all_gather | solution.py:67
  145.4 74.9 %while.11 = (s32[]{:T(128)}, f32[4,128,256]{1,2,0:T(8,128)S(1)}, pred[]{:T(512)}, bf16[32,128,256]{2,1,0:T(8,128)(2,1)}, bf16[32,128,256]{2,1,0:T(8,128)(2,1)}, ...) while((s32[]{:T(128)}, f32[4,128,256]{1,2,0:T(8,128)S(1)}, pred[]{:T(512)}, ...), condition=%wide.region_1.2_spmd.clone, body=%wide.region_0.1_spmd.clone.sunk | while | flops 202178560 | bytes 2032228 | solution.py:62
  146.3 1.4 fusion.28
  148.6 1.4 fusion.28
  151.0 1.4 fusion.28
  153.3 1.4 fusion.28
  155.7 1.4 fusion.28
  158.0 1.4 fusion.28
  160.4 1.4 fusion.28
  162.7 1.4 fusion.28
  165.0 1.4 fusion.28
  167.4 1.4 fusion.28
  169.7 1.4 fusion.28
  172.1 1.4 fusion.28
  174.4 1.4 fusion.28
  176.7 1.4 fusion.28
  179.1 1.4 fusion.28
  181.4 1.4 fusion.28
  183.8 1.4 fusion.28
  186.1 1.4 fusion.28
  188.4 1.4 fusion.28
  190.8 1.4 fusion.28
  193.1 1.4 fusion.28
  195.5 1.4 fusion.28
  197.8 1.4 fusion.28
  200.1 1.4 fusion.28
  202.5 1.4 fusion.28
  204.8 1.4 fusion.28
  207.2 1.4 fusion.28
  209.5 1.4 fusion.28
  211.9 1.4 fusion.28
  214.2 1.4 fusion.28
  216.5 1.4 fusion.28
  218.9 1.4 fusion.28
  220.5 3.1 collective-permute-start.1
  223.6 11.5 %collective-permute-done.1 = f32[4,128,256]{2,1,0:T(8,128)S(1)} collective-permute-done((f32[4,128,256]{2,1,0:T(8,128)S(1)}, f32[4,128,256]{2,1,0:T(8,128)S(1)}, u32[]{:S(2)}, u32[]{:S(2)}) %collective-permute-start.1) | collective-permute-done | bytes 524320 | tf_op jit(solution)/shard_map/ppermute | solution.py:12
  235.1 4.8 %collective-permute-start.2 = (f32[4,128,256]{2,1,0:T(8,128)S(1)}, f32[4,128,256]{2,1,0:T(8,128)S(1)}, u32[]{:S(2)}, u32[]{:S(2)}) collective-permute-start(f32[4,128,256]{2,1,0:T(8,128)S(1)} %broadcast_select_fusion), channel_id=1, source_target_pairs={{0,64},{32,96},{64,0},{96,32},{128,192},{160,224},{192,128},{224,1... | collective-permute-start | bytes 1572872 | tf_op jit(solution)/shard_map/ppermute | solution.py:12
  239.9 10.3 %collective-permute-done.2 = f32[4,128,256]{2,1,0:T(8,128)S(1)} collective-permute-done((f32[4,128,256]{2,1,0:T(8,128)S(1)}, f32[4,128,256]{2,1,0:T(8,128)S(1)}, u32[]{:S(2)}, u32[]{:S(2)}) %collective-permute-start.2) | collective-permute-done | bytes 524320 | tf_op jit(solution)/shard_map/ppermute | solution.py:12
  250.4 4.1 %collective-permute-start.3 = (f32[4,128,256]{2,1,0:T(8,128)S(1)}, f32[4,128,256]{2,1,0:T(8,128)S(1)}, u32[]{:S(2)}, u32[]{:S(2)}) collective-permute-start(f32[4,128,256]{2,1,0:T(8,128)S(1)} %broadcast_select_fusion.1), channel_id=1, source_target_pairs={{0,128},{32,160},{64,192},{96,224},{128,0},{160,32},{192,64},{224,... | collective-permute-start | bytes 1572872 | tf_op jit(solution)/shard_map/ppermute | solution.py:12
  254.5 23.2 %collective-permute-done.3 = f32[4,128,256]{2,1,0:T(8,128)S(1)} collective-permute-done((f32[4,128,256]{2,1,0:T(8,128)S(1)}, f32[4,128,256]{2,1,0:T(8,128)S(1)}, u32[]{:S(2)}, u32[]{:S(2)}) %collective-permute-start.3) | collective-permute-done | bytes 524320 | tf_op jit(solution)/shard_map/ppermute | solution.py:12
  277.7 2.7 collective-permute-start.4
  280.5 25.6 %collective-permute-done.4 = f32[4,128,256]{2,1,0:T(8,128)S(1)} collective-permute-done((f32[4,128,256]{2,1,0:T(8,128)S(1)}, f32[4,128,256]{2,1,0:T(8,128)S(1)}, u32[]{:S(2)}, u32[]{:S(2)}) %collective-permute-start.4) | collective-permute-done | bytes 524320 | tf_op jit(solution)/shard_map/ppermute | solution.py:12
  306.2 1.9 collective-permute-start.5
  308.4 6.8 %collective-permute-done.5 = f32[4,128,128]{2,1,0:T(8,128)S(1)} collective-permute-done((f32[4,128,128]{2,1,0:T(8,128)S(1)}, f32[4,128,128]{2,1,0:T(8,128)S(1)}, u32[]{:S(2)}, u32[]{:S(2)}) %collective-permute-start.5) | collective-permute-done | bytes 262176 | tf_op jit(solution)/shard_map/ppermute | solution.py:12
  (61 shorter events, 34.3 us)
Async XLA Ops:
  6.5 73.6 %all-gather.3.cloned.1.call-start = ((), (), s32[]{:S(2)}) async-start(), calls=%async_computation | async-start | bytes 2228224 | tf_op jit(solution)/shard_map/all_gather | solution.py:66
  7.3 138.2 %all-gather.5.cloned.1.call-start = ((), (), s32[]{:S(2)}) async-start(), calls=%async_computation.1 | async-start | bytes 2228224 | tf_op jit(solution)/shard_map/all_gather | solution.py:67
  7.3 6.6 %collective-permute-start = (bf16[2,128,256]{2,1,0:T(8,128)(2,1)}, bf16[2,128,256]{2,1,0:T(8,128)(2,1)S(1)}, u32[]{:S(2)}, u32[]{:S(2)}) collective-permute-start(bf16[2,128,256]{2,1,0:T(8,128)(2,1)} %param.9), channel_id=1, source_target_pairs={{0,1},{1,0},{2,3},{3,2},{4,5},{5,4},{6,7},{7,6},{8,9},{9,8},{10,11... | collective-permute-start | bytes 393224 | tf_op jit(solution)/shard_map/ppermute | solution.py:12
  13.9 0.7 copy-start
  220.5 14.5 %collective-permute-start.1 = (f32[4,128,256]{2,1,0:T(8,128)S(1)}, f32[4,128,256]{2,1,0:T(8,128)S(1)}, u32[]{:S(2)}, u32[]{:S(2)}) collective-permute-start(f32[4,128,256]{2,1,0:T(8,128)S(1)} %copy.24), channel_id=1, source_target_pairs={{0,32},{32,0},{64,96},{96,64},{128,160},{160,128},{192,224},{224,1... | collective-permute-start | bytes 1572872 | tf_op jit(solution)/shard_map/ppermute | solution.py:12
  223.6 56.9 %copy-start.1 = (f32[32]{0:T(128)S(1)}, f32[32]{0:T(128)}, u32[]{:S(2)}) copy-start(f32[32]{0:T(128)} %param.10) | copy-start | bytes 388
  235.1 15.1 %collective-permute-start.2 = (f32[4,128,256]{2,1,0:T(8,128)S(1)}, f32[4,128,256]{2,1,0:T(8,128)S(1)}, u32[]{:S(2)}, u32[]{:S(2)}) collective-permute-start(f32[4,128,256]{2,1,0:T(8,128)S(1)} %broadcast_select_fusion), channel_id=1, source_target_pairs={{0,64},{32,96},{64,0},{96,32},{128,192},{160,224},{192,128},{224,1... | collective-permute-start | bytes 1572872 | tf_op jit(solution)/shard_map/ppermute | solution.py:12
  250.3 57.9 %copy-start.2 = (f32[256]{0:T(256)S(1)}, f32[256]{0:T(256)}, u32[]{:S(2)}) copy-start(f32[256]{0:T(256)} %param.11) | copy-start | bytes 3076
  250.4 27.3 %collective-permute-start.3 = (f32[4,128,256]{2,1,0:T(8,128)S(1)}, f32[4,128,256]{2,1,0:T(8,128)S(1)}, u32[]{:S(2)}, u32[]{:S(2)}) collective-permute-start(f32[4,128,256]{2,1,0:T(8,128)S(1)} %broadcast_select_fusion.1), channel_id=1, source_target_pairs={{0,128},{32,160},{64,192},{96,224},{128,0},{160,32},{192,64},{224,... | collective-permute-start | bytes 1572872 | tf_op jit(solution)/shard_map/ppermute | solution.py:12
  277.7 28.4 %collective-permute-start.4 = (f32[4,128,256]{2,1,0:T(8,128)S(1)}, f32[4,128,256]{2,1,0:T(8,128)S(1)}, u32[]{:S(2)}, u32[]{:S(2)}) collective-permute-start(f32[4,128,256]{2,1,0:T(8,128)S(1)} %broadcast_select_fusion.2), channel_id=1, source_target_pairs={{0,256},{32,288},{64,320},{96,352},{128,384},{160,416},{192,448},{... | collective-permute-start | bytes 1572872 | tf_op jit(solution)/shard_map/ppermute | solution.py:12
  306.2 8.9 %collective-permute-start.5 = (f32[4,128,128]{2,1,0:T(8,128)S(1)}, f32[4,128,128]{2,1,0:T(8,128)S(1)}, u32[]{:S(2)}, u32[]{:S(2)}) collective-permute-start(f32[4,128,128]{2,1,0:T(8,128)S(1)} %constant_dynamic-slice_fusion), channel_id=1, source_target_pairs={{0,1},{1,0},{2,3},{3,2},{4,5},{5,4},{6,7},{7,6},{8,9},{9,8},{10,11... | collective-permute-start | bytes 786440 | tf_op jit(solution)/shard_map/ppermute | solution.py:12
Sparse Core Ops, SparseCore 0:
  10.4 69.7 all-gather.2
  83.2 62.1 all-gather.4
where the time goes:
time: 326 us; the launch traced here: 323 us
  waiting for transfers between devices  208 us (64%)
  matrix products  46.6 us (14%)
  other arithmetic  29.8 us (9%)
  starting transfers between devices  20.7 us (6%)
  between operations  13.6 us (4%)
  local copies, waits for them, and re-layouts  3.99 us (1%)
    ppermute x6, waiting for transfers between devices, partner_2(): return lax.ppermute(value, axis, pairs)  79.8 us
    all_gather x1, waiting for transfers between devices, on_device(): lax.all_gather(partner, 'ia', axis=0, tiled=True)  65.2 us
    all_gather x1, waiting for transfers between devices, on_device(): lax.all_gather(integrals, 'ia', axis=0, tiled=True)  61.7 us
    dot_general x32, matrix products, own_term(): jnp.einsum('ac,pcb->pab', mine, inner, preferred_element_type=jnp.float32)  45.5 us
    select_n x32, other arithmetic, full_rows(): lower = jnp.where(own_first, mine, other)  28.4 us
    ppermute x6, starting transfers between devices, partner_2(): return lax.ppermute(value, axis, pairs)  20.6 us
  transfers between devices with their start and end apart: 8, of which 8 were waited for; matrix products, arithmetic and copies ran while one was open for 1% of the time, Pallas kernels for 0%

commit v1 on v0

v1 whole, which is shorter than its diff:
```python
import jax
import jax.numpy as jnp
from jax import lax
from jax.experimental import pallas as pl
from jax.experimental.pallas import tpu as pltpu
from jax.sharding import PartitionSpec as P

NX, NY, NZ = 4, 8, 8
NT = 2
VB = 128
KT = 3
ROWS = 64
WIDE = 256
PAIRS = 4
MESH = pl.DeviceIdType.MESH
ROWS_BY_ROWS = (((1,), (1,)), ((), ()))


def xor(a, b, bits):
    total = 0
    for level in range(bits):
        unit = 2**level
        total = total + (a // unit % 2 + b // unit % 2) % 2 * unit
    return total


def kernel(
    ints, amps, codes, out, buf, inner, dense, mirror, mirror_codes,
    ysend, yrecv, xsend, xrecv, zsend, zrecv, csend, crecv, msend, mrecv, vsend, vrecv,
):
    ia, ja, v = lax.axis_index("ia"), lax.axis_index("ja"), lax.axis_index("vert")
    x, y = ia % NX, ia // NX * 2 + v
    z, core = ja // 2, ja % 2
    zp = z % 2

    def device(x_at, y_at, z_at, core_at):
        return (y_at // 2 * NX + x_at, z_at * 2 + core_at, y_at % 2)

    left, right, across = (x + 3) % NX, (x + 1) % NX, (x + 2) % NX
    to_left, to_right = device(left, y, z, core), device(right, y, z, core)
    to_down, to_up = device(x, y, (z + NZ - 1) % NZ, core), device(x, y, (z + 1) % NZ, core)
    to_core = device(x, y, z, 1 - core)
    to_vert = (ia, ja, 1 - v)
    to_mirror = (xor(ia, ja, 4), ja, v)
    to_column = [device(x, (y + d) % NY, z, core) for d in range(1, NY)]
    has_mirror = ja > 0

    def send(src, dst, send_sem, recv_sem, target):
        return pltpu.make_async_remote_copy(
            src_ref=src, dst_ref=dst, send_sem=send_sem, recv_sem=recv_sem,
            device_id=target, device_id_type=MESH,
        )

    barrier = pltpu.get_barrier_semaphore()
    for peer in [to_left, to_right, to_down, to_up, to_core, *to_column]:
        pl.semaphore_signal(barrier, inc=1, device_id=peer, device_id_type=MESH)

    @pl.when(has_mirror)
    def _():
        pl.semaphore_signal(barrier, inc=1, device_id=to_mirror, device_id_type=MESH)
        pl.semaphore_wait(barrier, 5 + NY)

    @pl.when(jnp.logical_not(has_mirror))
    def _():
        pl.semaphore_wait(barrier, 5 + NY - 1)

    share = 2 * zp + core
    other_share = 2 * (1 - zp) + core
    groups = [x, left, right, across]
    mine = ints.at[core, pl.ds(pl.multiple_of(zp * ROWS, ROWS), ROWS), :]

    column = [
        send(mine, buf.at[share, x, y], ysend.at[d], yrecv.at[d], to_column[d])
        for d in range(NY - 1)
    ]
    for d in (0, 6, 1, 5, 2, 4, 3):
        column[d].start()

    def chunk(half, j):
        return mirror.at[pl.ds(half * 6 + 3 * j, 3)]

    over = [
        send(amps.at[pl.ds(v * 6 + 3 * j, 3)], chunk(v, j), msend.at[j], mrecv.at[j], to_mirror)
        for j in range(2)
    ]
    over_codes = send(codes, mirror_codes, msend.at[2], mrecv.at[2], to_mirror)
    aside = [send(chunk(v, j), chunk(v, j), vsend.at[j], vrecv.at[j], to_vert) for j in range(2)]

    @pl.when(has_mirror)
    def _():
        over_codes.start()
        for copy in over:
            copy.start()

    @pl.when(jnp.logical_not(has_mirror))
    def _():
        mirror[...] = amps[...]
        mirror_codes[...] = codes[...]

    buf[share, x, y] = mine[...]
    out[...] = jnp.zeros_like(out)

    def placed(tiles, listing, pair, tile):
        total = None
        for k in range(KT):
            factor = jnp.where(listing[k : k + 1, :] == tile, 1.0, 0.0).astype(jnp.bfloat16)
            term = tiles[pair * KT + k] * factor
            total = term if total is None else total + term
        return total

    def place(pair, c, d):
        return (slice(c * VB, (c + 1) * VB), slice(pair * WIDE + d * VB, pair * WIDE + (d + 1) * VB))

    for pair in range(PAIRS):
        for c in range(NT):
            for d in range(NT):
                dense[place(pair, c, d)] = placed(amps, codes, pair, c * NT + d)

    def part(which, n, h):
        return buf.at[which, groups[n], pl.ds(4 * h, 4)]

    def along(n, h, index, target):
        return send(part(share, n, h), part(share, n, h), xsend.at[index], xrecv.at[index], target)

    along_x = [
        along(0, 0, 0, to_right), along(0, 1, 1, to_right),
        along(0, 0, 2, to_left), along(0, 1, 3, to_left),
        along(1, 0, 4, to_right), along(2, 1, 5, to_left),
    ]
    along_z = [
        send(part(share, n, h), part(share, n, h), zsend.at[2 * n + h], zrecv.at[2 * n + h],
             to_up if h == 0 else to_down)
        for n in range(4) for h in range(2)
    ]
    along_c = [
        send(part(which, n, h), part(which, n, h), csend.at[4 * n + 2 * s + h],
             crecv.at[4 * n + 2 * s + h], to_core)
        for n in range(4) for s, which in enumerate((share, other_share)) for h in range(2)
    ]

    def spread(n, h):
        along_z[2 * n + h].start()
        along_c[4 * n + h].start()

    def pass_on(n):
        for h in range(2):
            along_z[2 * n + h].wait_recv()
            along_c[4 * n + 2 + h].start()

    for copy in column:
        copy.wait_recv()
    for index in (0, 3, 1, 2):
        along_x[index].start()
    spread(0, 0)
    spread(0, 1)

    @pl.when(has_mirror)
    def _():
        for j in range(2):
            over[j].wait_recv()
            aside[j].start()

    along_x[0].wait_recv()
    along_x[4].start()
    spread(1, 0)
    along_x[3].wait_recv()
    along_x[5].start()
    spread(2, 1)
    along_x[1].wait_recv()
    spread(1, 1)
    along_x[2].wait_recv()
    spread(2, 0)
    pass_on(0)

    @pl.when(has_mirror)
    def _():
        over_codes.wait_recv()
        for j in range(2):
            aside[j].wait_recv()

    for i in range(2):
        for j in range(2):
            for c in range(NT):
                for d in range(NT):
                    at = place(i * 2 + j, c, d)
                    turned = placed(mirror, mirror_codes, j * 2 + i, d * NT + c)
                    total = dense[at].astype(jnp.float32) + turned.astype(jnp.float32).T
                    dense[at] = total.astype(jnp.bfloat16)

    def ladder(n):
        g = groups[n]
        for q in range(0, 8, 2):
            k, first = q // 4, q % 4
            rows = []
            for hi in (first, first + 1):
                rows += [buf[k, g, 2 * hi + v], buf[2 + k, g, 2 * hi + v]]
            rows = jnp.concatenate(rows, axis=0)
            for pair in range(PAIRS):
                part_inner = jnp.dot(
                    rows, dense[:, pair * WIDE : (pair + 1) * WIDE],
                    preferred_element_type=jnp.float32,
                ).astype(jnp.bfloat16)
                for s in range(2):
                    inner[pair * VB : (pair + 1) * VB, (q + s) * WIDE : (q + s + 1) * WIDE] = (
                        part_inner[s * VB : (s + 1) * VB]
                    )
        factors = []
        for q in range(8):
            k, hi = q // 4, q % 4
            factors.append(
                jnp.concatenate(
                    [buf[k, g, 2 * hi], buf[2 + k, g, 2 * hi],
                     buf[k, g, 2 * hi + 1], buf[2 + k, g, 2 * hi + 1]], axis=0,
                )
            )
        out[...] += lax.dot_general(
            inner[...], jnp.concatenate(factors, axis=1), ROWS_BY_ROWS,
            preferred_element_type=jnp.float32,
        )

    def from_core(n):
        for index in range(4):
            along_c[4 * n + index].wait_recv()

    from_core(0)
    ladder(0)
    along_x[4].wait_recv()
    spread(3, 0)
    along_x[5].wait_recv()
    spread(3, 1)
    pass_on(1)
    pass_on(2)
    from_core(1)
    ladder(1)
    pass_on(3)
    from_core(2)
    ladder(2)
    from_core(3)
    ladder(3)

    for copy in [*column, *along_x, *along_z, *along_c]:
        copy.wait_send()

    @pl.when(has_mirror)
    def _():
        for copy in [*over, over_codes, *aside]:
            copy.wait_send()


def on_device(amplitudes, tile_lists, integrals, occupied_energy, virtual_energy):
    occ_tile = amplitudes.shape[2]
    half_rows, width = integrals.shape[1:]
    tiles = amplitudes.reshape(PAIRS * KT, VB, VB)
    codes = jnp.broadcast_to(tile_lists.reshape(KT, 1), (KT, 128))
    codes = jnp.concatenate([codes, jnp.full((8 - KT, 128), -1, jnp.int32)], axis=0)
    vmem = pl.BlockSpec(memory_space=pltpu.VMEM)
    dma = pltpu.SemaphoreType.DMA
    symmetrized = pl.pallas_call(
        kernel,
        out_shape=jax.ShapeDtypeStruct((PAIRS * half_rows, width), jnp.float32),
        in_specs=[vmem] * 3,
        out_specs=vmem,
        scratch_shapes=[
            pltpu.VMEM((4, NX, NY, ROWS, WIDE), jnp.bfloat16),
            pltpu.VMEM((PAIRS * VB, 8 * WIDE), jnp.bfloat16),
            pltpu.VMEM((WIDE, PAIRS * WIDE), jnp.bfloat16),
            pltpu.VMEM((PAIRS * KT, VB, VB), jnp.bfloat16),
            pltpu.VMEM((8, 128), jnp.int32),
            dma((7,)), dma((7,)), dma((6,)), dma((6,)), dma((8,)), dma((8,)),
            dma((16,)), dma((16,)), dma((3,)), dma((3,)), dma((2,)), dma((2,)),
        ],
        compiler_params=pltpu.CompilerParams(
            collective_id=0, has_side_effects=True, vmem_limit_bytes=32 * 1024 * 1024
        ),
        name="ladder",
    )(integrals, tiles, codes)
    parity = lax.axis_index("vert")
    row_tile, code_tile = lax.axis_index("ia"), lax.axis_index("ja")
    occ_i = lax.dynamic_slice_in_dim(occupied_energy, row_tile * occ_tile, occ_tile)
    occ_j = lax.dynamic_slice_in_dim(
        occupied_energy, jnp.bitwise_xor(row_tile, code_tile) * occ_tile, occ_tile
    )
    virt_rows = lax.dynamic_slice_in_dim(virtual_energy, parity * half_rows, half_rows)
    denom = (
        virt_rows[None, None, :, None]
        + virtual_energy[None, None, None, :]
        - (occ_i[:, None, None, None] + occ_j[None, :, None, None])
    )
    result = symmetrized.reshape(occ_tile, occ_tile, half_rows, width) / denom
    return result.reshape(1, 1, occ_tile, occ_tile, half_rows, width).astype(jnp.bfloat16)


def solution(mesh):
    return jax.shard_map(
        on_device,
        mesh=mesh,
        in_specs=(
            P("ia", "ja", None, None, None, None),
            P("ia", "ja", None),
            P("ia", "vert", None),
            P(),
            P(),
        ),
        out_specs=P("ia", "ja", None, None, "vert", None),
        check_vma=False,
    )
```

time: 326 us -> 52.8 us (0.16)
  waiting for transfers between devices: 208 us -> 0 us
  Pallas kernels: 0 us -> 47.4 us
  matrix products: 46.6 us -> 0 us
  other arithmetic: 29.8 us -> 1.01 us
  starting transfers between devices: 20.7 us -> 0 us
  between operations: 13.6 us -> 0.07 us
    all_gather x2 -> x0, waiting for transfers between devices: 127 us -> none  [the longest x1 65.2 us: on_device(): lax.all_gather(partner, 'ia', axis=0, tiled=True)]
    ppermute x6 -> x0, waiting for transfers between devices: 79.8 us -> none  [partner_2(): return lax.ppermute(value, axis, pairs)]
    pallas_call x0 -> x1, Pallas kernels: none -> 47.4 us  [on_device(): pl.pallas_call(kernel, out_shape=jax.ShapeDtypeStruct((PAIRS * half_rows,...]
    dot_general x33 -> x0, matrix products: 46.6 us -> none  [the longest x32 45.5 us: own_term(): jnp.einsum('ac,pcb->pab', mine, inner, preferred_element_type=jnp.float32)]
    select_n x37 -> x0, other arithmetic: 28.7 us -> none  [the longest x32 28.4 us: full_rows(): lower = jnp.where(own_first, mine, other)]
    ppermute x6 -> x0, starting transfers between devices: 20.6 us -> none  [partner_2(): return lax.ppermute(value, axis, pairs)]
  transfers between devices with their start and end apart: 8 -> 0, of which waited for: 8 -> 0; matrix products, arithmetic and copies ran while one was open for 1% -> 0% of each run, Pallas kernels for 0% -> 0%
where the time goes in v1:
time: 52.8 us; the launch traced here: 52.6 us
  Pallas kernels  47.4 us (90%)
  local copies, waits for them, and re-layouts  4.07 us (8%)
  other arithmetic  1.01 us (2%)
    pallas_call x1, Pallas kernels, on_device(): pl.pallas_call(kernel, out_shape=jax.ShapeDtypeStruct((PAIRS * half_rows,...  47.4 us
    unnamed x9, local copies, waits for them, and re-layouts  3.32 us

profile of v1, /device:TPU:1, one launch (start us, length us, event | category | flops | bytes accessed | tf_op | source)
XLA Modules:
  0.0 52.6 jit_solution(16720495247949706053)
XLA Ops:
  0.0 1.3 %copy.7 = bf16[1,1,2,2,3,16384]{5,4,3,2,1,0:T(4,128)(2,1)S(1)} copy(bf16[1,1,2,2,3,16384]{5,3,4,2,1,0:T(2,128)(2,1)} %param.5) | data formatting | bytes 786432 | tf_op args[0]
  1.3 0.0 copy-start
  1.3 0.5 %reshape.90.amps = bf16[12,128,128]{2,1,0:T(8,128)(2,1)S(1)} reshape(bf16[1,1,2,2,3,16384]{5,4,3,2,1,0:T(4,128)(2,1)S(1)} %copy.7) | data formatting | bytes 786432 | tf_op jit(solution)/shard_map/reshape | solution.py:253
  1.9 0.0 copy-start.3
  1.9 0.6 %copy-done.3 = s32[1,1,3]{2,1,0:T(1,128)S(1)} copy-done((s32[1,1,3]{2,1,0:T(1,128)S(1)}, s32[1,1,3]{2,1,0:T(1,128)}, u32[]{:S(2)}) %copy-start.3) | copy-done | bytes 36
  2.5 0.1 concatenate.6.codes
  2.6 0.0 copy-done
  2.6 47.4 %ladder.1 = f32[512,256]{1,0:T(8,128)S(1)} custom-call(bf16[2,128,256]{2,1,0:T(8,128)(2,1)S(1)} %copy-done, bf16[12,128,128]{2,1,0:T(8,128)(2,1)S(1)} %reshape.90.amps, s32[8,128]{1,0:T(8,128)S(1)} %concatenate.6.codes), custom_call_target="tpu_custom_call" | custom-call | tf_op jit(solution)/shard_map/ladder/pallas_call | solution.py:258
  50.1 0.0 copy-start.1
  50.1 0.6 %copy-done.1 = f32[32]{0:T(128)S(1)} copy-done((f32[32]{0:T(128)S(1)}, f32[32]{0:T(128)}, u32[]{:S(2)}) %copy-start.1) | copy-done | bytes 152
  50.7 0.1 fusion
  50.8 0.1 broadcast_add_fusion.1
  50.9 0.0 copy-start.2
  50.9 0.7 %copy-done.2 = f32[256]{0:T(256)S(1)} copy-done((f32[256]{0:T(256)S(1)}, f32[256]{0:T(256)}, u32[]{:S(2)}) %copy-start.2) | copy-done | bytes 1048
  51.6 0.1 dynamic_slice.9
  51.6 0.1 broadcast_add_fusion
  51.7 0.9 %divide_convert_fusion = bf16[1,1,2,2,128,256]{5,4,3,2,1,0:T(8,128)(2,1)} fusion(f32[1,1,2,2,128,256]{5,4,3,2,1,0:T(8,128)S(1)} %bitcast.2, f32[2,2]{1,0:T(2,128)S(1)} %broadcast_add_fusion.1, f32[128,256]{1,0:T(8,128)S(1)} %broadcast_add_fusion), kind=kLoop, calls=%fused_computation | loop fusion | flops 393216 | bytes 917520 | tf_op jit(solution)/shard_map/convert_element_type | solution.py:290
  (1 shorter events, 0.0 us)
Async XLA Ops:
  1.3 1.3 %copy-start = (bf16[2,128,256]{2,1,0:T(8,128)(2,1)S(1)}, bf16[2,128,256]{2,1,0:T(8,128)(2,1)}, u32[]{:S(2)}) copy-start(bf16[2,128,256]{2,1,0:T(8,128)(2,1)} %ints.1) | copy-start | bytes 393220
  1.9 0.7 %copy-start.3 = (s32[1,1,3]{2,1,0:T(1,128)S(1)}, s32[1,1,3]{2,1,0:T(1,128)}, u32[]{:S(2)}) copy-start(s32[1,1,3]{2,1,0:T(1,128)} %param.6) | copy-start | bytes 40
  50.1 0.7 %copy-start.1 = (f32[32]{0:T(128)S(1)}, f32[32]{0:T(128)}, u32[]{:S(2)}) copy-start(f32[32]{0:T(128)} %param.8) | copy-start | bytes 388
  50.9 0.7 %copy-start.2 = (f32[256]{0:T(256)S(1)}, f32[256]{0:T(256)}, u32[]{:S(2)}) copy-start(f32[256]{0:T(256)} %param.9) | copy-start | bytes 3076

commit v2 on v0

v2 whole, which is shorter than its diff:
```python
import jax
import jax.numpy as jnp
from jax import lax
from jax.experimental import pallas as pl
from jax.experimental.pallas import tpu as pltpu
from jax.sharding import PartitionSpec as P

NX, NY = 4, 8
NT = 2
VB = 128
KT = 3
WIDE = 256
PAIRS = 4
HALF = VB // 2
MESH = pl.DeviceIdType.MESH
ROWS_BY_ROWS = (((1,), (1,)), ((), ()))

STAGES = [(0,), (1, 4), (2, 5), (3, 6), (7,)]
ORDER = [
    ("column", 0), ("relayout", None), ("mirror", 0), ("mirror", 1), ("prepare", None), ("column", 1),
    ("mirror", 2), ("sides", 0), ("column", 2), ("sides", 1), ("forward", 0), ("across", 0), ("column", 3),
    ("forward", 1), ("sides", 2), ("forward", 2), ("across", 1), ("column", 4), ("core", 0), ("core", 1),
    ("symmetrize", 0), ("ladder", 0), ("sides", 3), ("across", 2), ("core", 2), ("ladder", 2), ("sides", 4),
    ("symmetrize", 1), ("ladder", 1), ("across", 3), ("ladder", 3), ("across", 4), ("core", 3),
    ("ladder", 4), ("ladder", 5), ("ladder_own", 0), ("ladder_own", 1), ("drain", None), ("core", 4),
    ("ladder_other", 0), ("ladder_other", 1),
]


def slot_of(offset):
    return offset + offset // 4 * (11 - 2 * offset)


def xor(a, b, bits):
    total = 0
    for level in range(bits):
        unit = 2**level
        total = total + (a // unit % 2 + b // unit % 2) % 2 * unit
    return total


def kernel(
    ints, amps, lists, occ, virt, out, buf, inner, dense, raw, tiles, mirror, codes, mirror_codes,
    listing, occ_s, virt_v, scale, acc,
    local, ysend, yrecv, xsend, xrecv, csend, crecv, msend, mrecv, vsend, vrecv,
):
    ia, ja, v = lax.axis_index("ia"), lax.axis_index("ja"), lax.axis_index("vert")
    x, y = ia % NX, ia // NX * 2 + v
    z, core = ja // 2, ja % 2

    def device(x_at, y_at, z_at, core_at):
        return (y_at // 2 * NX + x_at, z_at * 2 + core_at, y_at % 2)

    to_right, to_left = device((x + 1) % NX, y, z, core), device((x + 3) % NX, y, z, core)
    to_next, to_back = device(x, (y + 1) % NY, z, core), device(x, (y + 7) % NY, z, core)
    to_core = device(x, y, z, 1 - core)
    to_vert = (ia, ja, 1 - v)
    partner = xor(ia, ja, 4)
    far = ja // 8 * (1 - ja // 4 % 2)
    w = v + far * (1 - 2 * v)
    to_mirror = (partner, ja, w)
    has_mirror = ja > 0

    barrier = pltpu.get_barrier_semaphore()
    peers = [to_right, to_left, to_next, to_back, to_core]
    for peer in peers:
        pl.semaphore_signal(barrier, inc=1, device_id=peer, device_id_type=MESH)

    @pl.when(has_mirror)
    def _():
        pl.semaphore_signal(barrier, inc=1, device_id=to_mirror, device_id_type=MESH)

    fetch = [
        pltpu.make_async_copy(amps.at[0, 0], raw, local.at[0]),
        pltpu.make_async_copy(lists, listing, local.at[1]),
        pltpu.make_async_copy(ints.at[core], buf.at[0, 0, 0], local.at[2]),
        pltpu.make_async_copy(ints.at[1 - core], buf.at[1, 0, 0], local.at[3]),
        pltpu.make_async_copy(occ, occ_s, local.at[4]),
        pltpu.make_async_copy(virt, virt_v.at[0], local.at[5]),
    ]
    for copy in fetch:
        copy.start()
    @pl.when(has_mirror)
    def _():
        pl.semaphore_wait(barrier, len(peers) + 1)

    @pl.when(jnp.logical_not(has_mirror))
    def _():
        pl.semaphore_wait(barrier, len(peers))

    def send(src, dst, send_sem, recv_sem, target):
        return pltpu.make_async_remote_copy(
            src_ref=src, dst_ref=dst, send_sem=send_sem, recv_sem=recv_sem,
            device_id=target, device_id_type=MESH,
        )

    def block(n, s, r):
        rows = pl.ds(r * HALF, HALF)
        return ints.at[core, rows] if n == s == 0 else buf.at[0, n, s, rows]

    def landing(n, s, r):
        return buf.at[0, n, s, pl.ds(r * HALF, HALF)]

    def along_y(src, dst, r, index, target):
        return send(block(0, src, r), landing(0, dst, r), ysend.at[index], yrecv.at[index], target)

    ahead = [[along_y((0, 4, 5)[st], 4 + st, r, 4 * st + r, to_next) for r in range(2)] for st in range(3)]
    behind = [[along_y(st, 1 + st, r, 4 * st + 2 + r, to_back) for r in range(2)] for st in range(3)]
    ahead.append([along_y(6, 7, 0, 12, to_next), None])
    behind.append([None, along_y(3, 7, 1, 13, to_back)])

    def along_x(n, m, s, r, target):
        index = (m - 1) * 16 + s * 2 + r
        return send(block(n, s, r), landing(m, s, r), xsend.at[index], xrecv.at[index], target)

    rightward = [[along_x(0, 1, s, r, to_right) for r in range(2)] for s in range(8)]
    leftward = [[along_x(0, 2, s, r, to_left) for r in range(2)] for s in range(8)]
    relay = [[along_x(1, 3, s, 0, to_right), along_x(2, 3, s, 1, to_left)] for s in range(8)]

    def along_c(n, s, r):
        st = [st for st, slots in enumerate(STAGES) if s in slots][0]
        there = buf.at[1, n, s, pl.ds(r * HALF, HALF)]
        send(landing(n, s, r), there, csend.at[st], crecv.at[st], to_core).start()

    def from_column(st):
        for r in range(2):
            for way, s in ((ahead, 3 + st), (behind, st)):
                if st and way[st - 1][r] is not None:
                    way[st - 1][r].wait_recv()
                if st < 4 and way[st][r] is not None:
                    way[st][r].start()
                if st in (0, 4) and way is not ahead:
                    s = STAGES[st][0]
                elif st in (0, 4):
                    continue
                rightward[s][r].start()
                leftward[s][r].start()
                if st:
                    along_c(0, s, r)

    def from_sides(st):
        for r in range(2):
            for s in STAGES[st]:
                rightward[s][r].wait_recv()
                if r == 0:
                    relay[s][r].start()
                along_c(1, s, r)
                leftward[s][r].wait_recv()
                if r == 1:
                    relay[s][r].start()
                along_c(2, s, r)

    def from_across(st):
        for r in range(2):
            for s in STAGES[st]:
                relay[s][r].wait_recv()
                along_c(3, s, r)

    def whole(st):
        here = buf.at[1, slice(0 if st else 1, 4), 0 : len(STAGES[st])]
        return send(here, here, csend.at[st], crecv.at[st], to_core)

    def from_core(st):
        whole(st).wait_recv()

    def chunk(half, k):
        return pl.ds(half * 6 + 2 * k, 2)

    over = [
        send(tiles.at[chunk(w, k)], mirror.at[chunk(w, k)], msend.at[k], mrecv.at[k], to_mirror)
        for k in range(KT)
    ]
    over_codes = send(codes, mirror_codes, msend.at[KT], mrecv.at[KT], to_mirror)
    aside = [
        send(mirror.at[chunk(v, k)], mirror.at[chunk(v, k)], vsend.at[k], vrecv.at[k], to_vert)
        for k in range(KT)
    ]

    def relayout(_):
        fetch[0].wait()
        for i in range(2):
            for k in range(KT):
                tiles[pl.ds((i * KT + k) * 2, 2)] = raw[i, k].reshape(2, VB, VB)
        fetch[1].wait()
        for k in range(KT):
            codes[k : k + 1, :] = jnp.broadcast_to(listing[0, :, k : k + 1], (1, 128))

    def send_mirror(k):
        @pl.when(has_mirror)
        def _():
            if k == 0:
                over_codes.start()
            over[k].start()

        @pl.when(jnp.logical_not(has_mirror))
        def _():
            mirror[4 * k : 4 * k + 4] = tiles[4 * k : 4 * k + 4]
            mirror_codes[...] = codes[...]

    def forward_mirror(k):
        @pl.when(has_mirror)
        def _():
            over[k].wait_recv()
            aside[k].start()

    def placed(tiles, listing, i, j, tile):
        total = None
        for k in range(KT):
            factor = jnp.where(listing[k : k + 1, :] == tile, 1.0, 0.0).astype(jnp.bfloat16)
            term = tiles[(i * KT + k) * 2 + j] * factor
            total = term if total is None else total + term
        return total

    def place(i, c, d):
        return (slice(c * VB, (c + 1) * VB), slice(i * WIDE + d * VB, i * WIDE + (d + 1) * VB))

    def prepare(_):
        for i in range(2):
            for j in range(2):
                for c in range(NT):
                    for d in range(NT):
                        dense[(j, *place(i, c, d))] = placed(tiles, codes, i, j, c * NT + d)
        fetch[4].wait()
        fetch[5].wait()
        every = virt_v[0:1, :]
        own = jnp.where(v == 0, every[:, :VB], every[:, VB:])
        down = jnp.broadcast_to(own, (VB, VB)).T
        virtual = jnp.concatenate([down, down], axis=1) + every
        for i in range(2):
            for j in range(2):
                energy = occ_s[ia * 2 + i] + occ_s[partner * 2 + j]
                scale[j, i * VB : (i + 1) * VB] = 1.0 / (virtual - energy)

    def symmetrize(part):
        h = v + part * (1 - 2 * v)

        @pl.when(has_mirror)
        def _():
            if part == 0:
                over_codes.wait_recv()
            else:
                for copy in aside:
                    copy.wait_recv()

        for i in range(2):
            for c in range(NT):
                for d in range(NT):
                    at = (h, *place(i, c, d))
                    turned = placed(mirror, mirror_codes, h, i, d * NT + c)
                    total = dense[at].astype(jnp.float32) + turned.astype(jnp.float32).T
                    dense[at] = total.astype(jnp.bfloat16)

    def product(e, h, ks):
        here = slot_of(2 * e % 8)
        low, high = slot_of((2 * e - v + 8) % 8), slot_of((2 * e + 1 - v) % 8)
        which = [(k, n) for k in ks for n in range(4)]
        for q in range(0, len(which), 2):
            rows = jnp.concatenate([buf[(*which[q], here)], buf[(*which[q + 1], here)]], axis=0)
            for i in range(2):
                part_inner = jnp.dot(
                    rows, dense[h, :, i * WIDE : (i + 1) * WIDE], preferred_element_type=jnp.float32
                ).astype(jnp.bfloat16)
                for s in range(2):
                    inner[i * VB : (i + 1) * VB, (q + s) * WIDE : (q + s + 1) * WIDE] = (
                        part_inner[s * VB : (s + 1) * VB]
                    )
        factors = [jnp.concatenate([buf[(*at, low)], buf[(*at, high)]], axis=0) for at in which]
        return lax.dot_general(
            inner[:, : len(which) * WIDE], jnp.concatenate(factors, axis=1), ROWS_BY_ROWS,
            preferred_element_type=jnp.float32,
        )

    def pairs(part):
        return v + part * (1 - 2 * v)

    def ladder(index):
        h, e = pairs(index % 2), [0, 3 - 2 * v, 1 + 2 * v][index // 2]
        if index == 0:
            fetch[2].wait()
            fetch[3].wait()
        term = product(e, h, (0, 1))
        acc[h] = term if index < 2 else acc[h] + term

    def ladder_own(part):
        h = pairs(part)
        acc[h] += product(2, h, (0,))

    def ladder_other(part):
        h = pairs(part)
        result = ((acc[h] + product(2, h, (1,))) * scale[h]).astype(jnp.bfloat16)
        for i in range(2):
            out[0, 0, i, h] = result[i * VB : (i + 1) * VB]

    def drain(_):
        for copies in [*ahead, *behind, *rightward, *leftward, *relay]:
            for copy in copies:
                if copy is not None:
                    copy.wait_send()
        for st in range(4):
            whole(st).wait_send()

        @pl.when(has_mirror)
        def _():
            for copy in [*over, over_codes, *aside]:
                copy.wait_send()

    steps = {
        "column": from_column, "sides": from_sides, "across": from_across, "core": from_core,
        "mirror": send_mirror, "forward": forward_mirror, "prepare": prepare,
        "symmetrize": symmetrize, "ladder": ladder, "ladder_own": ladder_own, "ladder_other": ladder_other,
        "relayout": relayout, "drain": drain,
    }
    for name, index in ORDER:
        steps[name](index)

    whole(4).wait_send()


def on_device(amplitudes, tile_lists, integrals, occupied_energy, virtual_energy):
    occ_tile = amplitudes.shape[2]
    half_rows, width = integrals.shape[1:]
    anywhere = pl.BlockSpec(memory_space=pl.ANY)
    dma = pltpu.SemaphoreType.DMA
    by_tile = amplitudes.transpose(0, 1, 2, 4, 3, 5)
    return pl.pallas_call(
        kernel,
        out_shape=jax.ShapeDtypeStruct((1, 1, occ_tile, occ_tile, half_rows, width), jnp.bfloat16),
        in_specs=[anywhere] * 5,
        out_specs=pl.BlockSpec(memory_space=pltpu.VMEM),
        scratch_shapes=[
            pltpu.VMEM((2, NX, NY, VB, WIDE), jnp.bfloat16),
            pltpu.VMEM((2 * VB, 8 * WIDE), jnp.bfloat16),
            pltpu.VMEM((2, WIDE, 2 * WIDE), jnp.bfloat16),
            pltpu.VMEM(by_tile.shape[2:], jnp.bfloat16),
            pltpu.VMEM((PAIRS * KT, VB, VB), jnp.bfloat16),
            pltpu.VMEM((PAIRS * KT, VB, VB), jnp.bfloat16),
            pltpu.VMEM((8, 128), jnp.int32),
            pltpu.VMEM((8, 128), jnp.int32),
            pltpu.VMEM(tile_lists.shape, jnp.int32),
            pltpu.SMEM(occupied_energy.shape, jnp.float32),
            pltpu.VMEM((8, WIDE), jnp.float32),
            pltpu.VMEM((2, 2 * VB, WIDE), jnp.float32),
            pltpu.VMEM((2, 2 * VB, WIDE), jnp.float32),
            dma((6,)), dma((14,)), dma((14,)), dma((48,)), dma((48,)), dma((5,)), dma((5,)),
            dma((KT + 1,)), dma((KT + 1,)), dma((KT,)), dma((KT,)),
        ],
        compiler_params=pltpu.CompilerParams(
            collective_id=0, has_side_effects=True, vmem_limit_bytes=60 * 1024 * 1024
        ),
        name="ladder",
    )(integrals, by_tile, tile_lists, occupied_energy, virtual_energy)


def solution(mesh):
    return jax.shard_map(
        on_device,
        mesh=mesh,
        in_specs=(
            P("ia", "ja", None, None, None, None),
            P("ia", "ja", None),
            P("ia", "vert", None),
            P(),
            P(),
        ),
        out_specs=P("ia", "ja", None, None, "vert", None),
        check_vma=False,
    )
```

time: 326 us -> 41.4 us (0.13)
  the two profiles are of different devices: /device:TPU:1 before, /device:TPU:321 now
where the time goes in v2:
time: 41.4 us; the launch traced here: 41.3 us
  Pallas kernels  39.6 us (96%)
  local copies, waits for them, and re-layouts  1.67 us (4%)
    pallas_call x1, Pallas kernels, on_device(): pl.pallas_call(kernel, out_shape=jax.ShapeDtypeStruct((1, 1, occ_tile, oc...  39.6 us
    unnamed x1, local copies, waits for them, and re-layouts  1.67 us

profile of v2, /device:TPU:321, one launch (start us, length us, event | category | flops | bytes accessed | tf_op | source)
XLA Modules:
  0.0 41.3 jit_solution(7159166195191036112)
XLA Ops:
  0.0 39.6 %ladder.1 = bf16[1,1,2,2,128,256]{5,4,3,2,1,0:T(8,128)(2,1)} custom-call(bf16[2,128,256]{2,1,0:T(8,128)(2,1)} %ints.1, bf16[1,1,2,3,2,16384]{5,4,3,2,1,0:T(2,128)(2,1)} %bitcast.1, s32[1,1,3]{2,1,0:T(1,128)} %lists.1, f32[32]{0:T(128)} %occ.1, f32[256]{0:T(256)} %virt.1), custom_call_target="tpu_custom_call" | custom-call | tf_op jit(solution)/shard_map/ladder/pallas_call | solution.py:325
  39.6 1.7 %copy.7 = bf16[1,1,2,2,128,256]{5,4,3,2,1,0:T(8,128)(2,1)} copy(bf16[1,1,2,2,128,256]{5,4,3,2,1,0:T(8,128)(2,1)} %ladder.1) | data formatting | bytes 524288

commit v3 on v2

--- a/solution.py
+++ b/solution.py
@@ -17,11 +17,11 @@
 
 STAGES = [(0,), (1, 4), (2, 5), (3, 6), (7,)]
 ORDER = [
-    ("column", 0), ("relayout", None), ("mirror", 0), ("mirror", 1), ("prepare", None), ("column", 1),
-    ("mirror", 2), ("sides", 0), ("column", 2), ("sides", 1), ("forward", 0), ("across", 0), ("column", 3),
-    ("forward", 1), ("sides", 2), ("forward", 2), ("across", 1), ("column", 4), ("core", 0), ("core", 1),
-    ("symmetrize", 0), ("ladder", 0), ("sides", 3), ("across", 2), ("core", 2), ("ladder", 2), ("sides", 4),
-    ("symmetrize", 1), ("ladder", 1), ("across", 3), ("ladder", 3), ("across", 4), ("core", 3),
+    ("column", 0), ("relayout", None), ("mirror", 0), ("prepare", None), ("column", 1), ("mirror", 1),
+    ("sides", 0), ("column", 2), ("mirror", 2), ("sides", 1), ("forward", 0), ("column", 3), ("across", 0),
+    ("sides", 2), ("forward", 1), ("column", 4), ("across", 1), ("forward", 2), ("core", 0), ("core", 1),
+    ("symmetrize", 0), ("sides", 3), ("across", 2), ("ladder", 0), ("sides", 4), ("core", 2), ("ladder", 2),
+    ("symmetrize", 1), ("across", 3), ("ladder", 1), ("ladder", 3), ("core", 3), ("across", 4),
     ("ladder", 4), ("ladder", 5), ("ladder_own", 0), ("ladder_own", 1), ("drain", None), ("core", 4),
     ("ladder_other", 0), ("ladder_other", 1),
 ]

time: 41.4 us -> 40.1 us (0.969)
  the two profiles are of different devices: /device:TPU:321 before, /device:TPU:328 now
where the time goes in v3:
time: 40.1 us; the launch traced here: 39.9 us
  Pallas kernels  38.2 us (95%)
  local copies, waits for them, and re-layouts  1.67 us (4%)
    pallas_call x1, Pallas kernels, on_device(): pl.pallas_call(kernel, out_shape=jax.ShapeDtypeStruct((1, 1, occ_tile, oc...  38.2 us
    unnamed x1, local copies, waits for them, and re-layouts  1.67 us

profile of v3, /device:TPU:328, one launch (start us, length us, event | category | flops | bytes accessed | tf_op | source)
XLA Modules:
  0.0 39.9 jit_solution(1828972221404746662)
XLA Ops:
  0.0 38.2 %ladder.1 = bf16[1,1,2,2,128,256]{5,4,3,2,1,0:T(8,128)(2,1)} custom-call(bf16[2,128,256]{2,1,0:T(8,128)(2,1)} %ints.1, bf16[1,1,2,3,2,16384]{5,4,3,2,1,0:T(2,128)(2,1)} %bitcast.1, s32[1,1,3]{2,1,0:T(1,128)} %lists.1, f32[32]{0:T(128)} %occ.1, f32[256]{0:T(256)} %virt.1), custom_call_target="tpu_custom_call" | custom-call | tf_op jit(solution)/shard_map/ladder/pallas_call | solution.py:325
  38.2 1.7 %copy.7 = bf16[1,1,2,2,128,256]{5,4,3,2,1,0:T(8,128)(2,1)} copy(bf16[1,1,2,2,128,256]{5,4,3,2,1,0:T(8,128)(2,1)} %ladder.1) | data formatting | bytes 524288

commit v4 on v3

--- a/solution.py
+++ b/solution.py
@@ -17,9 +17,9 @@
 
 STAGES = [(0,), (1, 4), (2, 5), (3, 6), (7,)]
 ORDER = [
-    ("column", 0), ("relayout", None), ("mirror", 0), ("prepare", None), ("column", 1), ("mirror", 1),
+    ("column", 0), ("relayout", None), ("mirror", 0), ("column", 1), ("mirror", 1), ("prepare", None),
     ("sides", 0), ("column", 2), ("mirror", 2), ("sides", 1), ("forward", 0), ("column", 3), ("across", 0),
-    ("sides", 2), ("forward", 1), ("column", 4), ("across", 1), ("forward", 2), ("core", 0), ("core", 1),
+    ("forward", 1), ("sides", 2), ("column", 4), ("forward", 2), ("across", 1), ("core", 0), ("core", 1),
     ("symmetrize", 0), ("sides", 3), ("across", 2), ("ladder", 0), ("sides", 4), ("core", 2), ("ladder", 2),
     ("symmetrize", 1), ("across", 3), ("ladder", 1), ("ladder", 3), ("core", 3), ("across", 4),
     ("ladder", 4), ("ladder", 5), ("ladder_own", 0), ("ladder_own", 1), ("drain", None), ("core", 4),

time: 40.1 us -> 40.1 us (level)
  no operation moved by 1% of the time
where the time goes in v4:
time: 40.1 us; the launch traced here: 39.9 us
  Pallas kernels  38.2 us (95%)
  local copies, waits for them, and re-layouts  1.67 us (4%)
    pallas_call x1, Pallas kernels, on_device(): pl.pallas_call(kernel, out_shape=jax.ShapeDtypeStruct((1, 1, occ_tile, oc...  38.2 us
    unnamed x1, local copies, waits for them, and re-layouts  1.67 us

profile of v4, /device:TPU:328, one launch (start us, length us, event | category | flops | bytes accessed | tf_op | source)
XLA Modules:
  0.0 39.9 jit_solution(8761629492083182811)
XLA Ops:
  0.0 38.2 %ladder.1 = bf16[1,1,2,2,128,256]{5,4,3,2,1,0:T(8,128)(2,1)} custom-call(bf16[2,128,256]{2,1,0:T(8,128)(2,1)} %ints.1, bf16[1,1,2,3,2,16384]{5,4,3,2,1,0:T(2,128)(2,1)} %bitcast.1, s32[1,1,3]{2,1,0:T(1,128)} %lists.1, f32[32]{0:T(128)} %occ.1, f32[256]{0:T(256)} %virt.1), custom_call_target="tpu_custom_call" | custom-call | tf_op jit(solution)/shard_map/ladder/pallas_call | solution.py:325
  38.2 1.7 %copy.7 = bf16[1,1,2,2,128,256]{5,4,3,2,1,0:T(8,128)(2,1)} copy(bf16[1,1,2,2,128,256]{5,4,3,2,1,0:T(8,128)(2,1)} %ladder.1) | data formatting | bytes 524288
